TPU v7x, 32 devices: a whole 2x2x4 slice. The times are simulated.
32 devices in a mesh: scen: 2 (over x), trade: 16 (over z, y, core).
Axes of the slice: x: 2, y: 2, z: 4, core: 2. Of those that a mesh axis runs over, the one named last changes fastest.
Arguments:
- coefficients: bfloat16 [32768, 256], P('trade'), may hold values from -0.375 to 0.375
- scenario_basis: bfloat16 [256, 16, 256], P('trade', None, 'scen'), parts along dimension 2, may hold values from -6 to 6
- trade_set: int32 [32768], P('trade'), may hold values from 0 to 1023, as said below
- option_flag: int32 [32768], P('trade'), may hold values 0 or 1
- margin_lag: int32 [1024], P('trade'), may hold values from 1 to 3
Outputs:
- exposure: float32 [1024, 16, 256], P('trade', None, 'scen'), parts along dimension 2
There are 2 independent parts, one for each index of `scen`. A program takes and returns all parts, laid end to end along the dimension named above; an argument that names none is the same for every part. Nothing has to cross between parts.
Inputs may be any that keep to these rules, and one draw needn't show every extreme that they name: `trade_set`: set j belongs to owner j // 64. The trades of one device (aligned blocks of 2048 trades) name at most 8 distinct sets of any one owner; in every draw each device names exactly 8 sets of some owner, and some owner has 8 of its sets named by every device.
All inputs are finite; a program needn't handle non-finite values. No bound on the sum of `option_flag` on one device may be relied on, other than what follows from the above.
Results may differ from a plain program's by a relative error of at most 0.0027.
Values may be sent and summed in bfloat16 or wider, within the bound.
A program may use at most 128 MiB of HBM per device.

v0:
```python
import jax
import jax.numpy as jnp
from jax import lax
from jax.sharding import PartitionSpec as P

SETS_DEV = 64
CAP = 8
LAG_MAX = 3


def collateralise(netted, margin_lag):
    collateral = jnp.zeros_like(netted)
    for offset in range(1, LAG_MAX + 1):
        shifted = jnp.concatenate([jnp.zeros_like(netted[:, :offset]), netted[:, :-offset]], axis=1)
        collateral = jnp.where((margin_lag == offset)[:, None, None], shifted, collateral)
    return jnp.maximum(netted - collateral, 0.0)


def body(coefficients, scenario_basis, trade_set, option_flag, margin_lag):
    device_count = lax.axis_size("trade")
    basis_whole = lax.all_gather(scenario_basis, "trade", axis=0, tiled=True)
    features = basis_whole.shape[0]
    dates = basis_whole.shape[1]
    scenarios = basis_whole.shape[2]
    columns = dates * scenarios
    basis_flat = basis_whole.reshape(features, columns)
    trades = coefficients.shape[0]
    block_rows = min(512, trades)
    block_count = trades // block_rows
    coef_blocks = coefficients.reshape(block_count, block_rows, features)
    flag_blocks = option_flag.reshape(block_count, block_rows)
    total_sets = SETS_DEV * device_count

    def contract_worth_matrix(fitted_weight_matrix, callable_marker_list):
        appraised_contracts = jnp.dot(
            fitted_weight_matrix, basis_flat, preferred_element_type=jnp.float32
        )
        return jnp.where(
            callable_marker_list[:, None] == 1,
            jnp.maximum(appraised_contracts, 0.0),
            appraised_contracts,
        ).astype(jnp.bfloat16)

    counts = jnp.zeros((total_sets,), jnp.int32).at[trade_set].add(1)
    present = (counts > 0).reshape(device_count, SETS_DEV)
    rank_table = jnp.cumsum(present.astype(jnp.int32), axis=1) - 1
    slot_count = device_count * CAP
    slot_table = jnp.arange(device_count, dtype=jnp.int32)[:, None] * CAP + rank_table
    trade_slot = slot_table.reshape(-1)[trade_set]
    local_index = jnp.broadcast_to(
        jnp.arange(SETS_DEV, dtype=jnp.int32)[None, :], (device_count, SETS_DEV)
    )
    target = jnp.where(present, slot_table, slot_count).reshape(-1)
    slot_sets = (
        jnp.full((slot_count,), float(SETS_DEV), jnp.float32)
        .at[target]
        .set(local_index.reshape(-1).astype(jnp.float32), mode="drop")
    )
    slot_blocks = trade_slot.reshape(block_count, block_rows)
    slot_numbers = jnp.arange(slot_count, dtype=jnp.int32)

    def tally_slots(cumulative_credit_risk, inputs):
        fitted_weight_matrix, slot_rows, callable_marker_list = inputs
        estimated_worth = contract_worth_matrix(fitted_weight_matrix, callable_marker_list)
        early_stop_choice = (slot_rows[None, :] == slot_numbers[:, None]).astype(jnp.bfloat16)
        return (
            cumulative_credit_risk
            + jnp.dot(early_stop_choice, estimated_worth, preferred_element_type=jnp.float32),
            None,
        )

    partial_sums, _ = lax.scan(
        tally_slots,
        jnp.zeros((slot_count, columns), jnp.float32),
        (coef_blocks, slot_blocks, flag_blocks),
    )
    received, received_sets = (
        lax.all_to_all(partial_sums, "trade", split_axis=0, concat_axis=0, tiled=True),
        lax.all_to_all(slot_sets[:, None], "trade", split_axis=0, concat_axis=0, tiled=True),
    )
    selector = (
        received_sets[:, 0][None, :] == jnp.arange(SETS_DEV, dtype=jnp.float32)[:, None]
    ).astype(jnp.float32)
    owned = jnp.dot(
        selector, received, precision=lax.Precision.HIGHEST, preferred_element_type=jnp.float32
    )
    netted = owned.reshape(SETS_DEV, dates, scenarios)
    return collateralise(netted, margin_lag)


def solution(mesh):
    placed = (P("trade", None), P("trade", None, "scen"), P("trade"), P("trade"), P("trade"))
    return jax.shard_map(
        body, mesh=mesh, in_specs=placed, out_specs=P("trade", None, "scen"), check_vma=False
    )
```

profile of v0, /device:TPU:0, one launch (start us, length us, event | category | flops | bytes accessed | tf_op | source)
XLA Modules:
  0.0 101.2 jit_solution(4699276855998185170)
XLA Ops:
  6.5 0.0 all-gather.2.cloned.1.call-start
  6.5 0.7 all-gather.2.cloned.1.call-update
  7.3 0.7 broadcast_clamp_fusion
  8.0 14.7 %scatter_custom_fusion = s32[1024]{0:T(1024)S(1)} fusion(s32[2048]{0:T(1024)S(1)} %get-tuple-element.81, s32[2048]{0:T(1024)S(1)} %broadcast.59, s32[]{:T(128)} %constant.6.clone.1), kind=kCustom, calls=%fused_computation.27 | custom fusion | flops 2048 | bytes 4100 | tf_op jit(solution)/shard_map/scatter-add | solution.py:44
  22.6 0.1 reshape.58
  22.7 0.2 reduce_window_sum.11
  22.9 0.1 add_add_fusion
  23.0 0.1 add.42
  23.1 0.1 reshape.79
  23.2 4.3 %scatter_custom_fusion.1 = f32[128]{0:T(128)S(1)} fusion(s32[1024]{0:T(1024)S(1)} %compare_select_fusion.1, f32[1024]{0:T(1024)S(1)} %reshape.79, f32[]{:T(128)} %constant.18.clone.1), kind=kCustom, calls=%fused_computation.33 | custom fusion | bytes 516 | tf_op jit(solution)/shard_map/scatter | solution.py:57
  27.5 0.7 all_to_all.14
  28.2 7.4 %all-to-all-start = ((f32[16,8,1]{1,2,0:T(1,128)}), f32[16,8,1]{1,2,0:T(1,128)S(1)}, u32[]{:S(2)}, u32[]{:S(2)}) async-start(f32[16,8,1]{1,2,0:T(1,128)} %bitcast), calls=%async_computation | async-start | bytes 16384 | tf_op jit(solution)/shard_map/all_to_all | solution.py:79
  35.6 0.0 copy-start
  35.6 8.6 %gather_fusion = s32[2048]{0:T(1024)S(1)} fusion(s32[1024]{0:T(1024)S(1)} %add.42, s32[2048]{0:T(1024)S(1)} %get-tuple-element.80), kind=kCustom, calls=%fused_computation | custom fusion | bytes 24576 | tf_op jit(solution)/shard_map/gather | solution.py:49
  44.2 0.0 copy-done
  44.2 6.1 %all-gather.2.cloned.1.call-done = bf16[256,16,128]{2,1,0:T(8,128)(2,1)} async-done(((bf16[16,16,128]{2,1,0:T(8,128)(2,1)}), bf16[256,16,128]{2,1,0:T(8,128)(2,1)}) %all-gather.2.cloned.1.call-update) | async-done | bytes 1048592 | tf_op jit(solution)/shard_map/all_gather | solution.py:21
  50.3 1.5 %copy.15 = bf16[32,8,16,128]{3,1,2,0:T(8,128)(2,1)S(1)} copy(bf16[32,8,16,128]{3,2,1,0:T(8,128)(2,1)} %bitcast.30) | data formatting | bytes 2097152
  51.8 13.3 %while.11 = (s32[]{:T(128)}, f32[128,2048]{1,0:T(8,128)}, s32[4,512]{1,0:T(4,128)S(1)}, s32[4,512]{1,0:T(4,128)S(1)}, bf16[4,512,256]{2,1,0:T(8,128)(2,1)}, /*in...) while((s32[]{:T(128)}, f32[128,2048]{1,0:T(8,128)}, s32[4,512]{1,0:T(4,128)S(1)}, ...), condition=%wide.region_4.5_spmd.clone, body=%wide.region_3.4_spmd.clone.sunk | while | flops 809042432 | bytes 3417703 | solution.py:72
  51.8 3.0 %convolution_add_fusion.2 = f32[128,2048]{1,0:T(8,128)} fusion(bf16[256,2048]{1,0:T(8,128)(2,1)S(1)} %get-tuple-element.143, pred[512]{0:T(512)(128)(4,1)S(1)} %compare_reduce_fusion.2, f32[128,2048]{1,0:T(8,128)} %get-tuple-element.131, pred[]{:T(512)S(6)} %compare.6, bf16[4,512,256]{2,1,0:T(8,128)(2,1)} %get-tuple-element.142, ...), kind=kOutput, calls=%fused_computation.6.clone.1 | convolution fusion | flops 809041920 | bytes 3410945 | tf_op jit(solution)/shard_map/while/body/eval_jaxpr/dot_general | solution.py:68
  54.9 3.4 %convolution_add_fusion.2 = f32[128,2048]{1,0:T(8,128)} fusion(bf16[256,2048]{1,0:T(8,128)(2,1)S(1)} %get-tuple-element.143, pred[512]{0:T(512)(128)(4,1)S(1)} %compare_reduce_fusion.2, f32[128,2048]{1,0:T(8,128)} %get-tuple-element.131, pred[]{:T(512)S(6)} %compare.6, bf16[4,512,256]{2,1,0:T(8,128)(2,1)} %get-tuple-element.142, ...), kind=kOutput, calls=%fused_computation.6.clone.1 | convolution fusion | flops 809041920 | bytes 3410945 | tf_op jit(solution)/shard_map/while/body/eval_jaxpr/dot_general | solution.py:68
  58.3 3.4 %convolution_add_fusion.2 = f32[128,2048]{1,0:T(8,128)} fusion(bf16[256,2048]{1,0:T(8,128)(2,1)S(1)} %get-tuple-element.143, pred[512]{0:T(512)(128)(4,1)S(1)} %compare_reduce_fusion.2, f32[128,2048]{1,0:T(8,128)} %get-tuple-element.131, pred[]{:T(512)S(6)} %compare.6, bf16[4,512,256]{2,1,0:T(8,128)(2,1)} %get-tuple-element.142, ...), kind=kOutput, calls=%fused_computation.6.clone.1 | convolution fusion | flops 809041920 | bytes 3410945 | tf_op jit(solution)/shard_map/while/body/eval_jaxpr/dot_general | solution.py:68
  61.7 3.4 %convolution_add_fusion.2 = f32[128,2048]{1,0:T(8,128)} fusion(bf16[256,2048]{1,0:T(8,128)(2,1)S(1)} %get-tuple-element.143, pred[512]{0:T(512)(128)(4,1)S(1)} %compare_reduce_fusion.2, f32[128,2048]{1,0:T(8,128)} %get-tuple-element.131, pred[]{:T(512)S(6)} %compare.6, bf16[4,512,256]{2,1,0:T(8,128)(2,1)} %get-tuple-element.142, ...), kind=kOutput, calls=%fused_computation.6.clone.1 | convolution fusion | flops 809041920 | bytes 3410945 | tf_op jit(solution)/shard_map/while/body/eval_jaxpr/dot_general | solution.py:68
  65.1 0.0 all-to-all-done
  65.1 0.0 copy-start.1
  65.1 3.8 %all-to-all-start.1 = ((f32[16,8,2048]{2,1,0:T(8,128)}), f32[16,8,2048]{2,1,0:T(8,128)S(1)}, u32[]{:S(2)}, u32[]{:S(2)}) async-start(f32[16,8,2048]{2,1,0:T(8,128)} %bitcast.3), calls=%async_computation.1 | async-start | bytes 2097152 | tf_op jit(solution)/shard_map/all_to_all | solution.py:78
  68.9 0.0 copy-done.1
  68.9 0.5 broadcast.93
  69.4 0.7 reduce.5
  70.1 0.1 eq.59
  70.2 21.6 %all-to-all-done.1 = f32[16,8,2048]{2,1,0:T(8,128)S(1)} async-done(((f32[16,8,2048]{2,1,0:T(8,128)}), f32[16,8,2048]{2,1,0:T(8,128)S(1)}, u32[]{:S(2)}, u32[]{:S(2)}) %all-to-all-start.1) | async-done | bytes 1048608 | tf_op jit(solution)/shard_map/all_to_all | solution.py:78
  91.8 0.3 copy.11
  92.1 0.7 fusion.12
  93.0 0.2 subtract_maximum_fusion
  93.2 1.1 %copy.12 = f32[64,16,128]{2,1,0:T(8,128)} copy(f32[64,16,128]{2,0,1:T(8,128)S(1)} %subtract_maximum_fusion) | data formatting | bytes 1048576 | tf_op jit(solution)/shard_map/max | solution.py:16
  (20 shorter events, 0.3 us)
Async XLA Ops:
  6.5 43.7 %all-gather.2.cloned.1.call-start = ((), (), s32[]{:S(2)}) async-start(), calls=%async_computation.2 | async-start | bytes 1114112 | tf_op jit(solution)/shard_map/all_gather | solution.py:21
  28.2 36.9 %all-to-all-start = ((f32[16,8,1]{1,2,0:T(1,128)}), f32[16,8,1]{1,2,0:T(1,128)S(1)}, u32[]{:S(2)}, u32[]{:S(2)}) async-start(f32[16,8,1]{1,2,0:T(1,128)} %bitcast), calls=%async_computation | async-start | bytes 16384 | tf_op jit(solution)/shard_map/all_to_all | solution.py:79
  35.6 8.6 %copy-start = (s32[2048]{0:T(1024)S(1)}, s32[2048]{0:T(1024)}, u32[]{:S(2)}) copy-start(s32[2048]{0:T(1024)} %param.10) | copy-start | bytes 24580
  65.1 3.8 %copy-start.1 = (s32[64]{0:T(128)S(1)}, s32[64]{0:T(128)}, u32[]{:S(2)}) copy-start(s32[64]{0:T(128)} %param.11) | copy-start | bytes 772
  65.1 26.7 %all-to-all-start.1 = ((f32[16,8,2048]{2,1,0:T(8,128)}), f32[16,8,2048]{2,1,0:T(8,128)S(1)}, u32[]{:S(2)}, u32[]{:S(2)}) async-start(f32[16,8,2048]{2,1,0:T(8,128)} %bitcast.3), calls=%async_computation.1 | async-start | bytes 2097152 | tf_op jit(solution)/shard_map/all_to_all | solution.py:78
Sparse Core Ops, SparseCore 0:
  9.5 40.7 all-gather.1
where the time goes:
time: 103 us; the launch traced here: 101 us
  waiting for transfers between devices  28.4 us (28%)
  local copies, waits for them, and re-layouts  17.5 us (17%)
  other arithmetic  16.7 us (16%)
  matrix products  13.9 us (13%)
  between operations  13.5 us (13%)
  starting transfers between devices  11.2 us (11%)
    all_to_all x1, waiting for transfers between devices, body(): lax.all_to_all(partial_sums, 'trade', split_axis=0, concat_axis=0, tiled=...  21.6 us
    scatter-add x1, other arithmetic, body(): counts = jnp.zeros((total_sets,), jnp.int32).at[trade_set].add(1)  14.7 us
    dot_general x4, matrix products, tally_slots(): jnp.dot(early_stop_choice, estimated_worth, preferred_element_type=jnp.fl...  13.1 us
    gather x1, local copies, waits for them, and re-layouts, body(): trade_slot = slot_table.reshape(-1)[trade_set]  8.58 us
    all_to_all x1, starting transfers between devices, body(): lax.all_to_all(slot_sets[:, None], 'trade', split_axis=0, concat_axis=0,...  7.39 us
    all_gather x1, waiting for transfers between devices, body(): basis_whole = lax.all_gather(scenario_basis, 'trade', axis=0, tiled=True)  6.07 us
    scatter x1, local copies, waits for them, and re-layouts, body(): slot_sets = jnp.full((slot_count,), float(SETS_DEV), jnp.float32).at[targ...  4.3 us
    all_to_all x1, starting transfers between devices, body(): lax.all_to_all(partial_sums, 'trade', split_axis=0, concat_axis=0, tiled=...  3.79 us
  transfers between devices with their start and end apart: 3, of which 2 were waited for; matrix products, arithmetic and copies ran while one was open for 44% of the time, Pallas kernels for 0%

commit v1 on v0

v1 whole, which is shorter than its diff:
```python
import functools

import jax
import jax.numpy as jnp
from jax import lax
from jax.experimental import pallas as pl
from jax.experimental.pallas import tpu as pltpu
from jax.sharding import PartitionSpec as P

SETS_DEV = 64
CAP = 8
LAG_MAX = 3
LANES = 128
INNER = 4
DATES_STEP = 4
ROWS_STEP = 512


def kernel(n, gathers, dates, coef_ref, basis_ref, set_ref, flag_ref, lag_ref, out_ref,
           whole, floor, member, sums, send, recv, ids_out, ids_in, lags_in, pick,
           bs_sem, br_sem, is_sem, ir_sem, ls_sem, lr_sem, ps_sem, pr_sem, *more):
    me = lax.axis_index("trade")
    slots = n * CAP
    trades = coef_ref.shape[0]
    steps = dates // DATES_STEP
    width = DATES_STEP * LANES

    def remote(src, dst, s_sem, r_sem, to):
        return pltpu.make_async_remote_copy(
            src_ref=src, dst_ref=dst, send_sem=s_sem, recv_sem=r_sem,
            device_id={"trade": to}, device_id_type=pl.DeviceIdType.MESH)

    def others(act):
        def go(k, carry):
            act(lax.rem(me + k, n))
            return carry
        lax.fori_loop(1, n, go, 0)

    barrier = pltpu.get_barrier_semaphore()
    others(lambda to: pl.semaphore_signal(
        barrier, inc=1, device_id={"trade": to}, device_id_type=pl.DeviceIdType.MESH))
    pl.semaphore_wait(barrier, n - 1)

    outer = n // INNER
    place, inner = me // INNER, lax.rem(me, INNER)
    core = lax.rem(inner, 2)
    sibling = place * INNER + inner - core + (1 - core)
    across = place * INNER + lax.rem(inner + 2, INNER)

    def block(owner, to, via):
        src = basis_ref if owner is me else whole.at[owner]
        return remote(src, whole.at[owner], bs_sem.at[via, owner], br_sem.at[owner], to)

    columns = [lax.rem(place + k, outer) for k in range(outer)]
    if gathers:
        for k in range(1, outer):
            block(me, columns[k] * INNER + inner, k - 1).start()
        block(me, across, outer - 1).start()
        block(me, sibling, outer).start()

    others(lambda to: remote(lag_ref, lags_in.at[me], ls_sem.at[to], lr_sem.at[me], to).start())
    lags_in[me] = lag_ref[...]
    if gathers:
        whole[me] = basis_ref[...]

    trade_set = set_ref[...]
    owner_row = trade_set // SETS_DEV
    local_row = trade_set - owner_row * SETS_DEV
    slot_of = lax.broadcasted_iota(jnp.int32, (slots, 1), 0)
    local_of = lax.broadcasted_iota(jnp.int32, (LANES, 1), 0)
    by_owner = (owner_row == slot_of // CAP).astype(jnp.float32).astype(jnp.bfloat16)
    by_local = (local_row == local_of).astype(jnp.float32).astype(jnp.bfloat16)
    counts = lax.dot_general(by_owner, by_local, (((1,), (1,)), ((), ())),
                             preferred_element_type=jnp.float32)
    present = counts > 0.5
    before = (lax.broadcasted_iota(jnp.int32, (LANES, LANES), 0)
              < lax.broadcasted_iota(jnp.int32, (LANES, LANES), 1))
    rank = jnp.dot(present.astype(jnp.float32).astype(jnp.bfloat16),
                   before.astype(jnp.float32).astype(jnp.bfloat16),
                   preferred_element_type=jnp.float32)
    chosen = present & (rank == lax.rem(slot_of, CAP).astype(jnp.float32))
    lane = lax.broadcasted_iota(jnp.int32, (slots, LANES), 1)
    local = jnp.sum(jnp.where(chosen, lane + 1, 0).astype(jnp.float32), axis=1, keepdims=True) - 1.0
    ids_out[...] = jnp.broadcast_to(local, (slots, LANES)).reshape(n, CAP, LANES)
    ids_in[me] = ids_out[me]
    others(lambda to: remote(
        ids_out.at[to], ids_in.at[me], is_sem.at[to], ir_sem.at[me], to).start())
    name = jnp.where(local < 0.0, -1, local.astype(jnp.int32) + (slot_of // CAP) * SETS_DEV)
    member[...] = (name == trade_set).astype(jnp.float32).astype(jnp.bfloat16)

    if gathers:
        for k in range(1, outer):
            owner = columns[k] * INNER + inner
            block(owner, owner, 0).wait_recv()
            block(owner, across, outer - 1).start()
            block(owner, sibling, outer).start()

    lowest = jnp.where(flag_ref[...] == 1, 0.0, -3.0e38).astype(jnp.float32)
    floor[...] = jnp.broadcast_to(lowest, (LANES, trades)).T

    others(lambda src: remote(
        lag_ref, lags_in.at[src], ls_sem.at[src], lr_sem.at[src], src).wait_recv())
    lag = jnp.sum(jnp.where(chosen, lags_in[...].reshape(slots, LANES), 0.0), axis=1, keepdims=True)
    lag = jnp.broadcast_to(lag, (slots, LANES))
    sums[0:LAG_MAX] = jnp.zeros((LAG_MAX, slots, LANES), jnp.float32)

    if gathers:
        for k in range(outer):
            owner = columns[k] * INNER + lax.rem(inner + 2, INNER)
            block(owner, owner, 0).wait_recv()
            block(owner, sibling, outer).start()

    others(lambda src: remote(
        ids_out.at[src], ids_in.at[src], is_sem.at[src], ir_sem.at[src], src).wait_recv())
    ids = ids_in[...]
    ids = jnp.concatenate([ids, ids], axis=1).reshape(n * 2 * CAP, LANES)
    row = lax.broadcasted_iota(jnp.int32, (n * 2 * CAP, LANES), 0)
    lane = lax.broadcasted_iota(jnp.int32, (n * 2 * CAP, LANES), 1)
    same = (lax.rem(row, 2 * CAP) // CAP) == lane // SETS_DEV
    hit = same & (ids == lax.rem(lane, SETS_DEV).astype(jnp.float32))
    pick[...] = jnp.where(hit, 1.0, 0.0).astype(jnp.float32).T.astype(jnp.bfloat16)

    if gathers:
        for pair in range(INNER // 2):
            for k in range(outer):
                owner = columns[k] * INNER + lax.rem(inner - core + (1 - core) + 2 * pair, INNER)
                block(owner, owner, 0).wait_recv()

    def basis_at(c):
        cols = pl.ds(pl.multiple_of(c * width, width), width)
        if gathers:
            return whole[:, :, cols].reshape(-1, width)
        return basis_ref[:, cols]

    def piece(c, to):
        return remote(send.at[c, to], recv.at[c, me], ps_sem.at[c, to], pr_sem.at[c, me], to)

    def step(c, carry):
        basis = basis_at(c)
        total = jnp.zeros((slots, width), jnp.float32)
        for first in range(0, trades, ROWS_STEP):
            rows = pl.ds(first, ROWS_STEP)
            valued = jnp.dot(coef_ref[rows, :], basis, preferred_element_type=jnp.float32)
            valued = jnp.maximum(valued, jnp.concatenate([floor[rows, :]] * DATES_STEP, axis=1))
            total += jnp.dot(member[:, rows], valued.astype(jnp.bfloat16),
                             preferred_element_type=jnp.float32)
        for d in range(DATES_STEP):
            sums[LAG_MAX + d] = total[:, d * LANES:(d + 1) * LANES]
        for half in range(DATES_STEP // 2):
            both = []
            for parity in range(2):
                at = LAG_MAX + 2 * half + parity
                collateral = jnp.zeros((slots, LANES), jnp.float32)
                for offset in range(1, LAG_MAX + 1):
                    collateral = jnp.where(lag == float(offset), sums[at - offset], collateral)
                both.append((sums[at] - collateral).reshape(n, CAP, LANES))
            send[c, :, half] = jnp.concatenate(both, axis=1).astype(jnp.bfloat16)
        for k in range(LAG_MAX):
            sums[k] = sums[DATES_STEP + k]
        recv[c, me] = send[c, me]
        others(lambda to: piece(c, to).start())
        return carry

    lax.fori_loop(0, steps, step, 0)

    def finish(c, carry):
        others(lambda src: remote(
            send.at[c, src], recv.at[c, src], ps_sem.at[c, src], pr_sem.at[c, src], src).wait_recv())
        for half in range(DATES_STEP // 2):
            result = jnp.dot(pick[...], recv[c, :, half].reshape(n * 2 * CAP, LANES),
                             preferred_element_type=jnp.float32)
            result = jnp.maximum(result, 0.0)
            for parity in range(2):
                at = pl.multiple_of((c * DATES_STEP + 2 * half + parity) * LANES, LANES)
                out_ref[:, pl.ds(at, LANES)] = result[parity * SETS_DEV:(parity + 1) * SETS_DEV]
        return carry

    lax.fori_loop(0, steps, finish, 0)

    if gathers:
        for k in range(1, outer):
            block(me, me, k - 1).wait_send()
        for k in range(outer):
            owner = columns[k] * INNER + inner
            block(owner, across, outer - 1).wait_send()
            block(owner, sibling, outer).wait_send()
            owner = columns[k] * INNER + lax.rem(inner + 2, INNER)
            block(owner, sibling, outer).wait_send()

    def sent(to):
        remote(lag_ref, lags_in.at[me], ls_sem.at[to], lr_sem.at[me], to).wait_send()
        remote(ids_out.at[to], ids_in.at[me], is_sem.at[to], ir_sem.at[me], to).wait_send()
        for c in range(steps):
            piece(c, to).wait_send()

    others(sent)


def body(coefficients, scenario_basis, trade_set, option_flag, margin_lag):
    n = lax.axis_size("trade")
    share, dates, scenarios = scenario_basis.shape
    trades, features = coefficients.shape
    columns = dates * scenarios
    gathers = share % 16 == 0 and n % INNER == 0
    basis = scenario_basis.reshape(share, columns)
    if not gathers:
        basis = lax.all_gather(basis, "trade", axis=0, tiled=True)
    lags = jnp.pad(margin_lag.astype(jnp.float32), (0, LANES - SETS_DEV))
    lags = jnp.broadcast_to(lags[None, :], (CAP, LANES))
    slots = n * CAP
    steps = dates // DATES_STEP
    halves = DATES_STEP // 2
    dma = pltpu.SemaphoreType.DMA
    whole = (n, share, columns) if gathers else (1, 16, LANES)
    out = pl.pallas_call(
        functools.partial(kernel, n, gathers, dates),
        out_shape=jax.ShapeDtypeStruct((SETS_DEV, columns), jnp.float32),
        in_specs=[pl.BlockSpec(memory_space=pltpu.VMEM)] * 5,
        out_specs=pl.BlockSpec(memory_space=pltpu.VMEM),
        scratch_shapes=[
            pltpu.VMEM(whole, jnp.bfloat16),
            pltpu.VMEM((trades, LANES), jnp.float32),
            pltpu.VMEM((slots, trades), jnp.bfloat16),
            pltpu.VMEM((LAG_MAX + DATES_STEP, slots, LANES), jnp.float32),
            pltpu.VMEM((steps, n, halves, 2 * CAP, LANES), jnp.bfloat16),
            pltpu.VMEM((steps, n, halves, 2 * CAP, LANES), jnp.bfloat16),
            pltpu.VMEM((n, CAP, LANES), jnp.float32),
            pltpu.VMEM((n, CAP, LANES), jnp.float32),
            pltpu.VMEM((n, CAP, LANES), jnp.float32),
            pltpu.VMEM((LANES, n * 2 * CAP), jnp.bfloat16),
            dma((n // INNER + 1, n)),
            dma((n,)),
            dma((n,)),
            dma((n,)),
            dma((n,)),
            dma((n,)),
            dma((steps, n)),
            dma((steps, n)),
        ],
        compiler_params=pltpu.CompilerParams(
            collective_id=0, has_side_effects=True, vmem_limit_bytes=48 * 1024 * 1024
        ),
        cost_estimate=pl.CostEstimate(
            flops=2 * trades * columns * (features + slots),
            bytes_accessed=4 * 1024 * 1024, transcendentals=0,
        ),
    )(coefficients, basis, trade_set[None, :], option_flag[None, :], lags)
    return out.reshape(SETS_DEV, dates, scenarios)


def solution(mesh):
    placed = (P("trade", None), P("trade", None, "scen"), P("trade"), P("trade"), P("trade"))
    return jax.shard_map(
        body, mesh=mesh, in_specs=placed, out_specs=P("trade", None, "scen"), check_vma=False
    )
```

time: 103 us -> 40 us (0.39); the launches traced: 101 us -> 39.8 us
  Pallas kernels: 0 us -> 36.1 us
  waiting for transfers between devices: 28.4 us -> 0 us
  other arithmetic: 16.7 us -> 0.01 us
  matrix products: 13.9 us -> 0 us
  local copies, waits for them, and re-layouts: 17.5 us -> 3.65 us
  between operations: 13.5 us -> 0.05 us
  starting transfers between devices: 11.2 us -> 0 us
    pallas_call x0 -> x1, Pallas kernels: none -> 36.1 us  [body(): pl.pallas_call(functools.partial(kernel, n, gathers, dates), out_shape=ja...]
    all_to_all x2 -> x0, waiting for transfers between devices: 21.6 us -> none  [the longest x1 21.6 us: body(): lax.all_to_all(partial_sums, 'trade', split_axis=0, concat_axis=0, tiled=...]
    scatter-add x1 -> x0, other arithmetic: 14.7 us -> none  [body(): counts = jnp.zeros((total_sets,), jnp.int32).at[trade_set].add(1)]
    dot_general x5 -> x0, matrix products: 13.9 us -> none  [the longest x4 13.1 us: tally_slots(): jnp.dot(early_stop_choice, estimated_worth, preferred_element_type=jnp.fl...]
    all_to_all x2 -> x0, starting transfers between devices: 11.2 us -> none  [the longest x1 7.39 us: body(): lax.all_to_all(slot_sets[:, None], 'trade', split_axis=0, concat_axis=0,...]
    gather x1 -> x0, local copies, waits for them, and re-layouts: 8.58 us -> none  [body(): trade_slot = slot_table.reshape(-1)[trade_set]]
    all_gather x1 -> x0, waiting for transfers between devices: 6.07 us -> none  [body(): basis_whole = lax.all_gather(scenario_basis, 'trade', axis=0, tiled=True)]
    scatter x1 -> x0, local copies, waits for them, and re-layouts: 4.3 us -> none  [body(): slot_sets = jnp.full((slot_count,), float(SETS_DEV), jnp.float32).at[targ...]
  transfers between devices with their start and end apart: 3 -> 0, of which waited for: 2 -> 0; matrix products, arithmetic and copies ran while one was open for 44% -> 0% of each run, Pallas kernels for 0% -> 0%
where the time goes in v1:
time: 40 us; the launch traced here: 39.8 us
  Pallas kernels  36.1 us (90%)
  local copies, waits for them, and re-layouts  3.65 us (9%)
    pallas_call x1, Pallas kernels, body(): pl.pallas_call(functools.partial(kernel, n, gathers, dates), out_shape=ja...  36.1 us
    unnamed x10, local copies, waits for them, and re-layouts  3.64 us

profile of v1, /device:TPU:0, one launch (start us, length us, event | category | flops | bytes accessed | tf_op | source)
XLA Modules:
  0.0 39.8 jit_solution(6393739373889286328)
XLA Ops:
  0.0 0.0 copy-start.3
  0.0 0.7 %copy-done.3 = s32[64]{0:T(128)S(1)} copy-done((s32[64]{0:T(128)S(1)}, s32[64]{0:T(128)}, u32[]{:S(2)}) %copy-start.3) | copy-done | bytes 280
  0.7 0.0 copy-start.1
  0.7 0.0 copy-start.2
  0.7 0.9 %copy.9 = bf16[2,8,16,128]{3,1,2,0:T(8,128)(2,1)S(1)} copy(bf16[2,8,16,128]{3,2,1,0:T(8,128)(2,1)} %bitcast.12) | data formatting | bytes 131072
  1.6 0.0 copy-done.1
  1.6 0.0 copy-done.2
  1.6 0.0 copy-start
  1.6 1.2 %copy-done = bf16[2048,256]{1,0:T(8,128)(2,1)S(1)} copy-done((bf16[2048,256]{1,0:T(8,128)(2,1)S(1)}, bf16[2048,256]{1,0:T(8,128)(2,1)}, u32[]{:S(2)}) %copy-start) | copy-done | bytes 1048600
  2.8 36.1 %shard_map.55 = f32[64,2048]{1,0:T(8,128)S(1)} custom-call(bf16[2048,256]{1,0:T(8,128)(2,1)S(1)} %copy-done, bf16[16,2048]{1,0:T(8,128)(2,1)S(1)} %bitcast.9, s32[1,2048]{1,0:T(1,128)S(1)} %bitcast.10, s32[1,2048]{1,0:T(1,128)S(1)} %bitcast.11, f32[8,128]{1,0:T(8,128)S(1)} %broadcast_in_dim.14.lag_ref), custom_call_target="tpu_custom_call" | custom-call | flops 3221225472 | bytes 4194304 | tf_op jit(solution)/shard_map/pallas_call | solution.py:215
  39.0 0.9 %copy.7 = f32[8,8,16,128]{3,2,1,0:T(8,128)} copy(f32[8,8,16,128]{3,1,2,0:T(8,128)S(1)} %bitcast.8) | data formatting | bytes 1048576
  (3 shorter events, 0.0 us)
Async XLA Ops:
  0.0 0.7 %copy-start.3 = (s32[64]{0:T(128)S(1)}, s32[64]{0:T(128)}, u32[]{:S(2)}) copy-start(s32[64]{0:T(128)} %param.9) | copy-start | bytes 772
  0.7 0.9 %copy-start.1 = (s32[2048]{0:T(1024)S(1)}, s32[2048]{0:T(1024)}, u32[]{:S(2)}) copy-start(s32[2048]{0:T(1024)} %param.7) | copy-start | bytes 24580
  0.7 0.9 %copy-start.2 = (s32[2048]{0:T(1024)S(1)}, s32[2048]{0:T(1024)}, u32[]{:S(2)}) copy-start(s32[2048]{0:T(1024)} %param.8) | copy-start | bytes 24580
  1.6 1.2 %copy-start = (bf16[2048,256]{1,0:T(8,128)(2,1)S(1)}, bf16[2048,256]{1,0:T(8,128)(2,1)}, u32[]{:S(2)}) copy-start(bf16[2048,256]{1,0:T(8,128)(2,1)} %coef_ref.1) | copy-start | bytes 3145732

commit v2 on v1

--- a/solution.py
+++ b/solution.py
@@ -13,18 +13,22 @@
 LANES = 128
 INNER = 4
 DATES_STEP = 4
-ROWS_STEP = 512
-
-
-def kernel(n, gathers, dates, coef_ref, basis_ref, set_ref, flag_ref, lag_ref, out_ref,
-           whole, floor, member, sums, send, recv, ids_out, ids_in, lags_in, pick,
-           bs_sem, br_sem, is_sem, ir_sem, ls_sem, lr_sem, ps_sem, pr_sem, *more):
+ROWS_STEP = 2048
+CUTS = 2
+
+
+def kernel(n, gathers, dates, coef_hbm, basis_ref, set_ref, flag_ref, lag_ref, out_ref,
+           coef_ref, coef_sem, whole, floor, member, sums, send, recv, ids_out, ids_in, lags_in, pick,
+           bs_sem, br_sem, is_sem, ir_sem, ls_sem, lr_sem, ps_sem, pr_sem):
     me = lax.axis_index("trade")
     slots = n * CAP
     trades = coef_ref.shape[0]
     steps = dates // DATES_STEP
     width = DATES_STEP * LANES
 
+    load = pltpu.make_async_copy(coef_hbm, coef_ref, coef_sem)
+    load.start()
+
     def remote(src, dst, s_sem, r_sem, to):
         return pltpu.make_async_remote_copy(
             src_ref=src, dst_ref=dst, send_sem=s_sem, recv_sem=r_sem,
@@ -47,16 +51,40 @@
     sibling = place * INNER + inner - core + (1 - core)
     across = place * INNER + lax.rem(inner + 2, INNER)
 
-    def block(owner, to, via):
-        src = basis_ref if owner is me else whole.at[owner]
-        return remote(src, whole.at[owner], bs_sem.at[via, owner], br_sem.at[owner], to)
+    cut = dates * LANES // CUTS
+
+    def block(part, owner, to, via):
+        cols = pl.ds(part * cut, cut)
+        src = basis_ref.at[:, cols] if owner is me else whole.at[owner, :, cols]
+        return remote(src, whole.at[owner, :, cols], bs_sem.at[part, via, owner],
+                      br_sem.at[part, owner], to)
+
+    def pass_columns(part):
+        for k in range(1, outer):
+            owner = columns[k] * INNER + inner
+            block(part, owner, owner, 0).wait_recv()
+            block(part, owner, across, outer - 1).start()
+            block(part, owner, sibling, outer).start()
+
+    def pass_across(part):
+        for k in range(outer):
+            owner = columns[k] * INNER + lax.rem(inner + 2, INNER)
+            block(part, owner, owner, 0).wait_recv()
+            block(part, owner, sibling, outer).start()
+
+    def end_gather(part):
+        for pair in range(INNER // 2):
+            for k in range(outer):
+                owner = columns[k] * INNER + lax.rem(inner - core + (1 - core) + 2 * pair, INNER)
+                block(part, owner, owner, 0).wait_recv()
 
     columns = [lax.rem(place + k, outer) for k in range(outer)]
     if gathers:
-        for k in range(1, outer):
-            block(me, columns[k] * INNER + inner, k - 1).start()
-        block(me, across, outer - 1).start()
-        block(me, sibling, outer).start()
+        for part in range(CUTS):
+            for k in range(1, outer):
+                block(part, me, columns[k] * INNER + inner, k - 1).start()
+            block(part, me, across, outer - 1).start()
+            block(part, me, sibling, outer).start()
 
     others(lambda to: remote(lag_ref, lags_in.at[me], ls_sem.at[to], lr_sem.at[me], to).start())
     lags_in[me] = lag_ref[...]
@@ -89,11 +117,7 @@
     member[...] = (name == trade_set).astype(jnp.float32).astype(jnp.bfloat16)
 
     if gathers:
-        for k in range(1, outer):
-            owner = columns[k] * INNER + inner
-            block(owner, owner, 0).wait_recv()
-            block(owner, across, outer - 1).start()
-            block(owner, sibling, outer).start()
+        pass_columns(0)
 
     lowest = jnp.where(flag_ref[...] == 1, 0.0, -3.0e38).astype(jnp.float32)
     floor[...] = jnp.broadcast_to(lowest, (LANES, trades)).T
@@ -105,10 +129,9 @@
     sums[0:LAG_MAX] = jnp.zeros((LAG_MAX, slots, LANES), jnp.float32)
 
     if gathers:
-        for k in range(outer):
-            owner = columns[k] * INNER + lax.rem(inner + 2, INNER)
-            block(owner, owner, 0).wait_recv()
-            block(owner, sibling, outer).start()
+        pass_across(0)
+        for part in range(1, CUTS):
+            pass_columns(part)
 
     others(lambda src: remote(
         ids_out.at[src], ids_in.at[src], is_sem.at[src], ir_sem.at[src], src).wait_recv())
@@ -120,11 +143,9 @@
     hit = same & (ids == lax.rem(lane, SETS_DEV).astype(jnp.float32))
     pick[...] = jnp.where(hit, 1.0, 0.0).astype(jnp.float32).T.astype(jnp.bfloat16)
 
-    if gathers:
-        for pair in range(INNER // 2):
-            for k in range(outer):
-                owner = columns[k] * INNER + lax.rem(inner - core + (1 - core) + 2 * pair, INNER)
-                block(owner, owner, 0).wait_recv()
+    load.wait()
+    if gathers:
+        end_gather(0)
 
     def basis_at(c):
         cols = pl.ds(pl.multiple_of(c * width, width), width)
@@ -161,7 +182,14 @@
         others(lambda to: piece(c, to).start())
         return carry
 
-    lax.fori_loop(0, steps, step, 0)
+    per_cut = steps // CUTS
+    for part in range(CUTS):
+        if gathers and part > 0:
+            end_gather(part)
+        lax.fori_loop(part * per_cut, part * per_cut + 1, step, 0)
+        if gathers and part + 1 < CUTS:
+            pass_across(part + 1)
+        lax.fori_loop(part * per_cut + 1, (part + 1) * per_cut, step, 0)
 
     def finish(c, carry):
         others(lambda src: remote(
@@ -178,14 +206,15 @@
     lax.fori_loop(0, steps, finish, 0)
 
     if gathers:
-        for k in range(1, outer):
-            block(me, me, k - 1).wait_send()
-        for k in range(outer):
-            owner = columns[k] * INNER + inner
-            block(owner, across, outer - 1).wait_send()
-            block(owner, sibling, outer).wait_send()
-            owner = columns[k] * INNER + lax.rem(inner + 2, INNER)
-            block(owner, sibling, outer).wait_send()
+        for part in range(CUTS):
+            for k in range(1, outer):
+                block(part, me, me, k - 1).wait_send()
+            for k in range(outer):
+                owner = columns[k] * INNER + inner
+                block(part, owner, across, outer - 1).wait_send()
+                block(part, owner, sibling, outer).wait_send()
+                owner = columns[k] * INNER + lax.rem(inner + 2, INNER)
+                block(part, owner, sibling, outer).wait_send()
 
     def sent(to):
         remote(lag_ref, lags_in.at[me], ls_sem.at[to], lr_sem.at[me], to).wait_send()
@@ -215,9 +244,11 @@
     out = pl.pallas_call(
         functools.partial(kernel, n, gathers, dates),
         out_shape=jax.ShapeDtypeStruct((SETS_DEV, columns), jnp.float32),
-        in_specs=[pl.BlockSpec(memory_space=pltpu.VMEM)] * 5,
+        in_specs=[pl.BlockSpec(memory_space=pl.ANY)] + [pl.BlockSpec(memory_space=pltpu.VMEM)] * 4,
         out_specs=pl.BlockSpec(memory_space=pltpu.VMEM),
         scratch_shapes=[
+            pltpu.VMEM((trades, features), jnp.bfloat16),
+            dma(()),
             pltpu.VMEM(whole, jnp.bfloat16),
             pltpu.VMEM((trades, LANES), jnp.float32),
             pltpu.VMEM((slots, trades), jnp.bfloat16),
@@ -228,8 +259,8 @@
             pltpu.VMEM((n, CAP, LANES), jnp.float32),
             pltpu.VMEM((n, CAP, LANES), jnp.float32),
             pltpu.VMEM((LANES, n * 2 * CAP), jnp.bfloat16),
-            dma((n // INNER + 1, n)),
-            dma((n,)),
+            dma((CUTS, n // INNER + 1, n)),
+            dma((CUTS, n)),
             dma((n,)),
             dma((n,)),
             dma((n,)),

time: 40 us -> 39.3 us (0.982)
  Pallas kernels: 36.1 us -> 35.4 us
    pallas_call x1, Pallas kernels: 36.1 us -> 35.4 us  [body(): pl.pallas_call(functools.partial(kernel, n, gathers, dates), out_shape=ja...]
where the time goes in v2:
time: 39.3 us; the launch traced here: 39.1 us
  Pallas kernels  35.4 us (90%)
  local copies, waits for them, and re-layouts  3.65 us (9%)
    pallas_call x1, Pallas kernels, body(): pl.pallas_call(functools.partial(kernel, n, gathers, dates), out_shape=ja...  35.4 us
    unnamed x10, local copies, waits for them, and re-layouts  3.64 us

profile of v2, /device:TPU:0, one launch (start us, length us, event | category | flops | bytes accessed | tf_op | source)
XLA Modules:
  0.0 39.1 jit_solution(15227374287566909892)
XLA Ops:
  0.0 0.0 copy-start.3
  0.0 0.7 %copy-done.3 = s32[64]{0:T(128)S(1)} copy-done((s32[64]{0:T(128)S(1)}, s32[64]{0:T(128)}, u32[]{:S(2)}) %copy-start.3) | copy-done | bytes 280
  0.7 0.0 copy-start.1
  0.7 0.0 copy-start.2
  0.7 0.9 %copy.9 = bf16[2,8,16,128]{3,1,2,0:T(8,128)(2,1)S(1)} copy(bf16[2,8,16,128]{3,2,1,0:T(8,128)(2,1)} %bitcast.12) | data formatting | bytes 131072
  1.6 0.0 copy-done.1
  1.6 0.0 copy-done.2
  1.6 0.0 copy-start
  1.6 1.2 %copy-done = bf16[2048,256]{1,0:T(8,128)(2,1)S(1)} copy-done((bf16[2048,256]{1,0:T(8,128)(2,1)S(1)}, bf16[2048,256]{1,0:T(8,128)(2,1)}, u32[]{:S(2)}) %copy-start) | copy-done | bytes 1048600
  2.8 35.4 %shard_map.55 = f32[64,2048]{1,0:T(8,128)S(1)} custom-call(bf16[2048,256]{1,0:T(8,128)(2,1)S(1)} %copy-done, bf16[16,2048]{1,0:T(8,128)(2,1)S(1)} %bitcast.9, s32[1,2048]{1,0:T(1,128)S(1)} %bitcast.10, s32[1,2048]{1,0:T(1,128)S(1)} %bitcast.11, f32[8,128]{1,0:T(8,128)S(1)} %broadcast_in_dim.14.lag_ref), custom_call_target="tpu_custom_call" | custom-call | flops 3221225472 | bytes 4194304 | tf_op jit(solution)/shard_map/pallas_call | solution.py:244
  38.2 0.9 %copy.7 = f32[8,8,16,128]{3,2,1,0:T(8,128)} copy(f32[8,8,16,128]{3,1,2,0:T(8,128)S(1)} %bitcast.8) | data formatting | bytes 1048576
  (3 shorter events, 0.0 us)
Async XLA Ops:
  0.0 0.7 %copy-start.3 = (s32[64]{0:T(128)S(1)}, s32[64]{0:T(128)}, u32[]{:S(2)}) copy-start(s32[64]{0:T(128)} %param.9) | copy-start | bytes 772
  0.7 0.9 %copy-start.1 = (s32[2048]{0:T(1024)S(1)}, s32[2048]{0:T(1024)}, u32[]{:S(2)}) copy-start(s32[2048]{0:T(1024)} %param.7) | copy-start | bytes 24580
  0.7 0.9 %copy-start.2 = (s32[2048]{0:T(1024)S(1)}, s32[2048]{0:T(1024)}, u32[]{:S(2)}) copy-start(s32[2048]{0:T(1024)} %param.8) | copy-start | bytes 24580
  1.6 1.2 %copy-start = (bf16[2048,256]{1,0:T(8,128)(2,1)S(1)}, bf16[2048,256]{1,0:T(8,128)(2,1)}, u32[]{:S(2)}) copy-start(bf16[2048,256]{1,0:T(8,128)(2,1)} %coef_hbm.1) | copy-start | bytes 3145732

commit v3 on v2

--- a/solution.py
+++ b/solution.py
@@ -18,8 +18,8 @@
 
 
 def kernel(n, gathers, dates, coef_hbm, basis_ref, set_ref, flag_ref, lag_ref, out_ref,
-           coef_ref, coef_sem, whole, floor, member, sums, send, recv, ids_out, ids_in, lags_in, pick,
-           bs_sem, br_sem, is_sem, ir_sem, ls_sem, lr_sem, ps_sem, pr_sem):
+           coef_ref, coef_sem, whole, floor, member, sums, send, recv, notes_out, notes_in, pick,
+           bs_sem, br_sem, ns_sem, nr_sem, ps_sem, pr_sem):
     me = lax.axis_index("trade")
     slots = n * CAP
     trades = coef_ref.shape[0]
@@ -43,8 +43,6 @@
     barrier = pltpu.get_barrier_semaphore()
     others(lambda to: pl.semaphore_signal(
         barrier, inc=1, device_id={"trade": to}, device_id_type=pl.DeviceIdType.MESH))
-    pl.semaphore_wait(barrier, n - 1)
-
     outer = n // INNER
     place, inner = me // INNER, lax.rem(me, INNER)
     core = lax.rem(inner, 2)
@@ -77,19 +75,6 @@
             for k in range(outer):
                 owner = columns[k] * INNER + lax.rem(inner - core + (1 - core) + 2 * pair, INNER)
                 block(part, owner, owner, 0).wait_recv()
-
-    columns = [lax.rem(place + k, outer) for k in range(outer)]
-    if gathers:
-        for part in range(CUTS):
-            for k in range(1, outer):
-                block(part, me, columns[k] * INNER + inner, k - 1).start()
-            block(part, me, across, outer - 1).start()
-            block(part, me, sibling, outer).start()
-
-    others(lambda to: remote(lag_ref, lags_in.at[me], ls_sem.at[to], lr_sem.at[me], to).start())
-    lags_in[me] = lag_ref[...]
-    if gathers:
-        whole[me] = basis_ref[...]
 
     trade_set = set_ref[...]
     owner_row = trade_set // SETS_DEV
@@ -109,33 +94,47 @@
     chosen = present & (rank == lax.rem(slot_of, CAP).astype(jnp.float32))
     lane = lax.broadcasted_iota(jnp.int32, (slots, LANES), 1)
     local = jnp.sum(jnp.where(chosen, lane + 1, 0).astype(jnp.float32), axis=1, keepdims=True) - 1.0
-    ids_out[...] = jnp.broadcast_to(local, (slots, LANES)).reshape(n, CAP, LANES)
-    ids_in[me] = ids_out[me]
-    others(lambda to: remote(
-        ids_out.at[to], ids_in.at[me], is_sem.at[to], ir_sem.at[me], to).start())
+    notes_out[:, 0:CAP] = jnp.broadcast_to(local, (slots, LANES)).reshape(n, CAP, LANES)
+    notes_out[:, CAP:2 * CAP] = jnp.broadcast_to(lag_ref[...][None], (n, CAP, LANES))
+    notes_in[me] = notes_out[me]
     name = jnp.where(local < 0.0, -1, local.astype(jnp.int32) + (slot_of // CAP) * SETS_DEV)
     member[...] = (name == trade_set).astype(jnp.float32).astype(jnp.bfloat16)
 
     if gathers:
-        pass_columns(0)
+        whole[me] = basis_ref[...]
 
     lowest = jnp.where(flag_ref[...] == 1, 0.0, -3.0e38).astype(jnp.float32)
     floor[...] = jnp.broadcast_to(lowest, (LANES, trades)).T
 
-    others(lambda src: remote(
-        lag_ref, lags_in.at[src], ls_sem.at[src], lr_sem.at[src], src).wait_recv())
-    lag = jnp.sum(jnp.where(chosen, lags_in[...].reshape(slots, LANES), 0.0), axis=1, keepdims=True)
-    lag = jnp.broadcast_to(lag, (slots, LANES))
     sums[0:LAG_MAX] = jnp.zeros((LAG_MAX, slots, LANES), jnp.float32)
 
-    if gathers:
+    pl.semaphore_wait(barrier, n - 1)
+    columns = [lax.rem(place + k, outer) for k in range(outer)]
+    if gathers:
+        for part in range(CUTS):
+            for k in range(1, outer):
+                block(part, me, columns[k] * INNER + inner, k - 1).start()
+            block(part, me, across, outer - 1).start()
+            block(part, me, sibling, outer).start()
+
+    def notes(to):
+        return remote(notes_out.at[to], notes_in.at[me], ns_sem, nr_sem, to)
+
+    others(lambda to: notes(to).start())
+    if gathers:
+        pass_columns(0)
         pass_across(0)
         for part in range(1, CUTS):
             pass_columns(part)
 
-    others(lambda src: remote(
-        ids_out.at[src], ids_in.at[src], is_sem.at[src], ir_sem.at[src], src).wait_recv())
-    ids = ids_in[...]
+    all_notes = remote(notes_out.at[pl.ds(0, n - 1)], notes_in.at[pl.ds(0, n - 1)],
+                       ns_sem, nr_sem, sibling)
+    all_notes.wait_recv()
+    known = notes_in[...]
+    lag = jnp.sum(jnp.where(chosen, known[:, CAP:].reshape(slots, LANES), 0.0),
+                  axis=1, keepdims=True)
+    lag = jnp.broadcast_to(lag, (slots, LANES))
+    ids = known[:, :CAP]
     ids = jnp.concatenate([ids, ids], axis=1).reshape(n * 2 * CAP, LANES)
     row = lax.broadcasted_iota(jnp.int32, (n * 2 * CAP, LANES), 0)
     lane = lax.broadcasted_iota(jnp.int32, (n * 2 * CAP, LANES), 1)
@@ -154,7 +153,11 @@
         return basis_ref[:, cols]
 
     def piece(c, to):
-        return remote(send.at[c, to], recv.at[c, me], ps_sem.at[c, to], pr_sem.at[c, me], to)
+        return remote(send.at[c, to], recv.at[c, me], ps_sem.at[c], pr_sem.at[c], to)
+
+    def pieces(c):
+        most = pl.ds(0, n - 1)
+        return remote(send.at[c, most], recv.at[c, most], ps_sem.at[c], pr_sem.at[c], sibling)
 
     def step(c, carry):
         basis = basis_at(c)
@@ -192,8 +195,7 @@
         lax.fori_loop(part * per_cut + 1, (part + 1) * per_cut, step, 0)
 
     def finish(c, carry):
-        others(lambda src: remote(
-            send.at[c, src], recv.at[c, src], ps_sem.at[c, src], pr_sem.at[c, src], src).wait_recv())
+        pieces(c).wait_recv()
         for half in range(DATES_STEP // 2):
             result = jnp.dot(pick[...], recv[c, :, half].reshape(n * 2 * CAP, LANES),
                              preferred_element_type=jnp.float32)
@@ -216,13 +218,9 @@
                 owner = columns[k] * INNER + lax.rem(inner + 2, INNER)
                 block(part, owner, sibling, outer).wait_send()
 
-    def sent(to):
-        remote(lag_ref, lags_in.at[me], ls_sem.at[to], lr_sem.at[me], to).wait_send()
-        remote(ids_out.at[to], ids_in.at[me], is_sem.at[to], ir_sem.at[me], to).wait_send()
-        for c in range(steps):
-            piece(c, to).wait_send()
-
-    others(sent)
+    all_notes.wait_send()
+    for c in range(steps):
+        pieces(c).wait_send()
 
 
 def body(coefficients, scenario_basis, trade_set, option_flag, margin_lag):
@@ -255,18 +253,15 @@
             pltpu.VMEM((LAG_MAX + DATES_STEP, slots, LANES), jnp.float32),
             pltpu.VMEM((steps, n, halves, 2 * CAP, LANES), jnp.bfloat16),
             pltpu.VMEM((steps, n, halves, 2 * CAP, LANES), jnp.bfloat16),
-            pltpu.VMEM((n, CAP, LANES), jnp.float32),
-            pltpu.VMEM((n, CAP, LANES), jnp.float32),
-            pltpu.VMEM((n, CAP, LANES), jnp.float32),
+            pltpu.VMEM((n, 2 * CAP, LANES), jnp.float32),
+            pltpu.VMEM((n, 2 * CAP, LANES), jnp.float32),
             pltpu.VMEM((LANES, n * 2 * CAP), jnp.bfloat16),
             dma((CUTS, n // INNER + 1, n)),
             dma((CUTS, n)),
-            dma((n,)),
-            dma((n,)),
-            dma((n,)),
-            dma((n,)),
-            dma((steps, n)),
-            dma((steps, n)),
+            dma(()),
+            dma(()),
+            dma((steps,)),
+            dma((steps,)),
         ],
         compiler_params=pltpu.CompilerParams(
             collective_id=0, has_side_effects=True, vmem_limit_bytes=48 * 1024 * 1024

time: 39.3 us -> 36.6 us (0.931)
  Pallas kernels: 35.4 us -> 32.7 us
    pallas_call x1, Pallas kernels: 35.4 us -> 32.7 us  [body(): pl.pallas_call(functools.partial(kernel, n, gathers, dates), out_shape=ja...]
where the time goes in v3:
time: 36.6 us; the launch traced here: 36.4 us
  Pallas kernels  32.7 us (89%)
  local copies, waits for them, and re-layouts  3.65 us (10%)
    pallas_call x1, Pallas kernels, body(): pl.pallas_call(functools.partial(kernel, n, gathers, dates), out_shape=ja...  32.7 us
    unnamed x10, local copies, waits for them, and re-layouts  3.64 us

profile of v3, /device:TPU:0, one launch (start us, length us, event | category | flops | bytes accessed | tf_op | source)
XLA Modules:
  0.0 36.4 jit_solution(7220173410819539495)
XLA Ops:
  0.0 0.0 copy-start.3
  0.0 0.7 %copy-done.3 = s32[64]{0:T(128)S(1)} copy-done((s32[64]{0:T(128)S(1)}, s32[64]{0:T(128)}, u32[]{:S(2)}) %copy-start.3) | copy-done | bytes 280
  0.7 0.0 copy-start.1
  0.7 0.0 copy-start.2
  0.7 0.9 %copy.9 = bf16[2,8,16,128]{3,1,2,0:T(8,128)(2,1)S(1)} copy(bf16[2,8,16,128]{3,2,1,0:T(8,128)(2,1)} %bitcast.12) | data formatting | bytes 131072
  1.6 0.0 copy-done.1
  1.6 0.0 copy-done.2
  1.6 0.0 copy-start
  1.6 1.2 %copy-done = bf16[2048,256]{1,0:T(8,128)(2,1)S(1)} copy-done((bf16[2048,256]{1,0:T(8,128)(2,1)S(1)}, bf16[2048,256]{1,0:T(8,128)(2,1)}, u32[]{:S(2)}) %copy-start) | copy-done | bytes 1048600
  2.8 32.7 %shard_map.55 = f32[64,2048]{1,0:T(8,128)S(1)} custom-call(bf16[2048,256]{1,0:T(8,128)(2,1)S(1)} %copy-done, bf16[16,2048]{1,0:T(8,128)(2,1)S(1)} %bitcast.9, s32[1,2048]{1,0:T(1,128)S(1)} %bitcast.10, s32[1,2048]{1,0:T(1,128)S(1)} %bitcast.11, f32[8,128]{1,0:T(8,128)S(1)} %broadcast_in_dim.14.lag_ref), custom_call_target="tpu_custom_call" | custom-call | flops 3221225472 | bytes 4194304 | tf_op jit(solution)/shard_map/pallas_call | solution.py:242
  35.5 0.9 %copy.7 = f32[8,8,16,128]{3,2,1,0:T(8,128)} copy(f32[8,8,16,128]{3,1,2,0:T(8,128)S(1)} %bitcast.8) | data formatting | bytes 1048576
  (3 shorter events, 0.0 us)
Async XLA Ops:
  0.0 0.7 %copy-start.3 = (s32[64]{0:T(128)S(1)}, s32[64]{0:T(128)}, u32[]{:S(2)}) copy-start(s32[64]{0:T(128)} %param.9) | copy-start | bytes 772
  0.7 0.9 %copy-start.1 = (s32[2048]{0:T(1024)S(1)}, s32[2048]{0:T(1024)}, u32[]{:S(2)}) copy-start(s32[2048]{0:T(1024)} %param.7) | copy-start | bytes 24580
  0.7 0.9 %copy-start.2 = (s32[2048]{0:T(1024)S(1)}, s32[2048]{0:T(1024)}, u32[]{:S(2)}) copy-start(s32[2048]{0:T(1024)} %param.8) | copy-start | bytes 24580
  1.6 1.2 %copy-start = (bf16[2048,256]{1,0:T(8,128)(2,1)S(1)}, bf16[2048,256]{1,0:T(8,128)(2,1)}, u32[]{:S(2)}) copy-start(bf16[2048,256]{1,0:T(8,128)(2,1)} %coef_hbm.1) | copy-start | bytes 3145732

commit v4 on v3

--- a/solution.py
+++ b/solution.py
@@ -12,7 +12,7 @@
 LAG_MAX = 3
 LANES = 128
 INNER = 4
-DATES_STEP = 4
+DATES_STEP = 8
 ROWS_STEP = 2048
 CUTS = 2
 
@@ -120,9 +120,10 @@
     def notes(to):
         return remote(notes_out.at[to], notes_in.at[me], ns_sem, nr_sem, to)
 
+    if gathers:
+        pass_columns(0)
     others(lambda to: notes(to).start())
     if gathers:
-        pass_columns(0)
         pass_across(0)
         for part in range(1, CUTS):
             pass_columns(part)

time: 36.6 us -> 36.3 us (level)
  no operation moved by 1% of the time
where the time goes in v4:
time: 36.3 us; the launch traced here: 36.1 us
  Pallas kernels  32.4 us (89%)
  local copies, waits for them, and re-layouts  3.65 us (10%)
    pallas_call x1, Pallas kernels, body(): pl.pallas_call(functools.partial(kernel, n, gathers, dates), out_shape=ja...  32.4 us
    unnamed x10, local copies, waits for them, and re-layouts  3.64 us

profile of v4, /device:TPU:0, one launch (start us, length us, event | category | flops | bytes accessed | tf_op | source)
XLA Modules:
  0.0 36.1 jit_solution(15896920454045952487)
XLA Ops:
  0.0 0.0 copy-start.3
  0.0 0.7 %copy-done.3 = s32[64]{0:T(128)S(1)} copy-done((s32[64]{0:T(128)S(1)}, s32[64]{0:T(128)}, u32[]{:S(2)}) %copy-start.3) | copy-done | bytes 280
  0.7 0.0 copy-start.1
  0.7 0.0 copy-start.2
  0.7 0.9 %copy.9 = bf16[2,8,16,128]{3,1,2,0:T(8,128)(2,1)S(1)} copy(bf16[2,8,16,128]{3,2,1,0:T(8,128)(2,1)} %bitcast.12) | data formatting | bytes 131072
  1.6 0.0 copy-done.1
  1.6 0.0 copy-done.2
  1.6 0.0 copy-start
  1.6 1.2 %copy-done = bf16[2048,256]{1,0:T(8,128)(2,1)S(1)} copy-done((bf16[2048,256]{1,0:T(8,128)(2,1)S(1)}, bf16[2048,256]{1,0:T(8,128)(2,1)}, u32[]{:S(2)}) %copy-start) | copy-done | bytes 1048600
  2.8 32.4 %shard_map.55 = f32[64,2048]{1,0:T(8,128)S(1)} custom-call(bf16[2048,256]{1,0:T(8,128)(2,1)S(1)} %copy-done, bf16[16,2048]{1,0:T(8,128)(2,1)S(1)} %bitcast.9, s32[1,2048]{1,0:T(1,128)S(1)} %bitcast.10, s32[1,2048]{1,0:T(1,128)S(1)} %bitcast.11, f32[8,128]{1,0:T(8,128)S(1)} %broadcast_in_dim.14.lag_ref), custom_call_target="tpu_custom_call" | custom-call | flops 3221225472 | bytes 4194304 | tf_op jit(solution)/shard_map/pallas_call | solution.py:243
  35.2 0.9 %copy.7 = f32[8,8,16,128]{3,2,1,0:T(8,128)} copy(f32[8,8,16,128]{3,1,2,0:T(8,128)S(1)} %bitcast.8) | data formatting | bytes 1048576
  (3 shorter events, 0.0 us)
Async XLA Ops:
  0.0 0.7 %copy-start.3 = (s32[64]{0:T(128)S(1)}, s32[64]{0:T(128)}, u32[]{:S(2)}) copy-start(s32[64]{0:T(128)} %param.9) | copy-start | bytes 772
  0.7 0.9 %copy-start.1 = (s32[2048]{0:T(1024)S(1)}, s32[2048]{0:T(1024)}, u32[]{:S(2)}) copy-start(s32[2048]{0:T(1024)} %param.7) | copy-start | bytes 24580
  0.7 0.9 %copy-start.2 = (s32[2048]{0:T(1024)S(1)}, s32[2048]{0:T(1024)}, u32[]{:S(2)}) copy-start(s32[2048]{0:T(1024)} %param.8) | copy-start | bytes 24580
  1.6 1.2 %copy-start = (bf16[2048,256]{1,0:T(8,128)(2,1)S(1)}, bf16[2048,256]{1,0:T(8,128)(2,1)}, u32[]{:S(2)}) copy-start(bf16[2048,256]{1,0:T(8,128)(2,1)} %coef_hbm.1) | copy-start | bytes 3145732
